TPU v7x, 32 devices: a whole 2x2x4 slice. The times are simulated.
32 devices in a mesh: seq: 8 (over z, y), dp: 4 (over x, core).
Axes of the slice: x: 2, y: 2, z: 4, core: 2. Of those that a mesh axis runs over, the one named last changes fastest.
Arguments:
- layer_rows: bfloat16 [4, 1024, 1024], P('dp', 'seq'), may hold values from -6 to 6
- doc_ids: int32 [4, 1024], P('dp', 'seq'), may hold values from 0 to 5, never falling along the last dimension, each value on 1 to 512 neighbouring positions
- packing: int32 [4, 8], P('dp'), may hold values from 0 to 7, each once within a row
- norm_gain: float32 [1024], replicated, may hold values from 0.1 to 1.9
- w_qkv: bfloat16 [1024, 3072], replicated, may hold values from -0.1875 to 0.1875
- d_attn: bfloat16 [4, 1024, 1024], P('dp', 'seq'), may hold values from -6 to 6
Outputs:
- d_input: bfloat16 [4, 1024, 1024], P('dp', 'seq')
- w_grad: float32 [1024, 3072], P('seq')
Inputs may be any that keep to these rules, and one draw needn't show every extreme that they name: `doc_ids`: in each group the song numbers never fall along the initial order; every number occurs, and one song spans exactly 512 frames. `packing`: each group's row names every block number once.
All inputs are finite; a program needn't handle non-finite values.
Results may differ from a plain program's by a relative error of at most 0.024.
Values may be sent and summed in bfloat16 or wider, within the bound.
A program may use at most 128 MiB of HBM per device.

v0:
```python
import functools
import math

import jax
import jax.numpy as jnp
from jax import lax
from jax.experimental import pallas as pl
from jax.experimental.pallas import tpu as pltpu
from jax.sharding import PartitionSpec as P

HEADS = 8
HEAD = 128
BLOCK = 128
DOCS = 6
EPS = 1e-05
FACTOR = 1.0 / math.sqrt(HEAD)
MESH = pl.DeviceIdType.MESH
VMEM_LIMIT = 56 * 1024 * 1024
CHUNKS = 4
NT = (((1,), (1,)), ((), ()))
TN = (((0,), (0,)), ((), ()))


def remote(src, dst, send, recv, **where):
    return pltpu.make_async_remote_copy(
        src_ref=src, dst_ref=dst, send_sem=send, recv_sem=recv, device_id=where, device_id_type=MESH
    )


def normalized(frames, gain):
    values = frames.astype(jnp.float32)
    inverse = lax.rsqrt(jnp.mean(values * values, axis=-1, keepdims=True) + EPS)
    unit = values * inverse
    return inverse, unit, (unit * gain).astype(jnp.bfloat16)


def halvings(rows, groups):
    sizes = []
    for _ in range(groups.bit_length() - 1):
        halved = rows % 32 == 0
        rows = rows // 2 if halved else rows
        sizes.append((rows, halved))
    return sizes


def kernel(
    n, groups, packing, frames, gain, w_qkv, docs, grads, d_out, w_all,
    frames_s, docs_s, grads_s, weights_s, normed_s, q_s, k_s, v_s, dk_s, dv_s,
    g_s, g_send, g_all, w_part, chosen, d_s, own_sem, *scratch,
):
    sizes = halvings(w_part.shape[1], groups)
    count = len(sizes)
    landed, sums = scratch[:count], scratch[count : 2 * count]
    zs, zr, ys, yr, ds, dr, ts, tr, gs, gr, hs, hr, ws, wr, ps, pr, bs, br = scratch[2 * count :]
    me = lax.axis_index("seq")
    dp = lax.axis_index("dp")
    side = lax.rem(me, 2)
    place = me // 2
    partner = me + 1 - 2 * side
    length = n // 2
    part = BLOCK // CHUNKS
    head = lax.rem(me, HEADS)
    peers = [lax.rem(me + k, n) for k in range(1, n)]
    bits = [lax.rem(dp // (1 << b), 2) for b in range(count)]
    partners = [dp + (1 << b) * (1 - 2 * bits[b]) for b in range(count)]

    def head_of(device):
        start = pl.multiple_of(lax.rem(device, HEADS) * HEAD, HEAD)
        return grads.at[:, pl.ds(start, HEAD)]

    barrier = pltpu.get_barrier_semaphore()
    for peer in peers:
        pl.semaphore_signal(barrier, inc=1, device_id={"seq": peer}, device_id_type=MESH)
    for other in partners:
        pl.semaphore_signal(barrier, inc=1, device_id={"dp": other}, device_id_type=MESH)
    own_frames = pltpu.make_async_copy(frames, frames_s.at[me], own_sem.at[0])
    own_weights = pltpu.make_async_copy(w_qkv, weights_s, own_sem.at[1])
    own_grads = pltpu.make_async_copy(head_of(me), grads_s.at[me], own_sem.at[2])
    own_docs = pltpu.make_async_copy(docs, docs_s.at[me], own_sem.at[3])
    for copy in (own_frames, own_weights, own_grads, own_docs):
        copy.start()
    pl.semaphore_wait(barrier, n - 1 + count)

    def piece(block, chunk):
        return frames_s.at[block, pl.ds(chunk * part, part), :]

    def along(way, hop, chunk, block, source=None):
        return remote(
            piece(block, chunk) if source is None else source, piece(block, chunk),
            zs.at[way, hop, chunk], zr.at[way, hop, chunk], seq=me + (2 if way == 0 else -2),
        )

    def across(way, hop, chunk, block, source=None):
        return remote(
            piece(block, chunk) if source is None else source, piece(block, chunk),
            ys.at[way, hop, chunk], yr.at[way, hop, chunk], seq=partner,
        )

    def can_send(way, hop):
        if way == 0:
            return (place + 1 < length) & (place - hop >= 0)
        return (place - 1 >= 0) & (place + hop < length)

    def arrives(way, hop):
        return place - 1 - hop >= 0 if way == 0 else place + 1 + hop < length

    def origin(way, hop):
        return me - 2 * (hop + 1) if way == 0 else me + 2 * (hop + 1)

    for chunk in range(CHUNKS):
        source = frames.at[pl.ds(chunk * part, part), :]
        for way in range(2):
            @pl.when(can_send(way, 0))
            def _():
                along(way, 0, chunk, me, source).start()
        across(0, 0, chunk, me, source).start()
    small = []
    for k in range(1, n):
        small.append(remote(docs, docs_s.at[me], ds.at[k - 1], dr.at[k - 1], seq=peers[k - 1]))
        small.append(
            remote(head_of(peers[k - 1]), grads_s.at[me], ts.at[k - 1], tr.at[k - 1], seq=peers[k - 1])
        )
    for copy in small:
        copy.start()

    def project(block):
        rows = pl.ds(pl.multiple_of(block * BLOCK, BLOCK), BLOCK)
        normed = normalized(frames_s[block], gain[...])[2]
        normed_s[rows, :] = normed
        for j, kept in enumerate((q_s, k_s, v_s)):
            columns = pl.ds(pl.multiple_of((j * HEADS + head) * HEAD, HEAD), HEAD)
            kept[rows, :] = jnp.dot(
                normed, weights_s[:, columns], preferred_element_type=jnp.float32
            ).astype(jnp.bfloat16)

    order = packing[...]
    for r in range(n):
        for b in range(n):
            chosen[r * n + b] = jnp.broadcast_to(
                jnp.where(order[:, r : r + 1] == b, 1.0, 0.0), (1, HEAD)
            )
    own_frames.wait()
    own_weights.wait()
    project(me)
    for hop in range(length - 1):
        for chunk in range(CHUNKS):
            for way in range(2):
                @pl.when(arrives(way, hop))
                def _():
                    block = origin(way, hop)
                    along(way, hop, chunk, block).wait_recv()
                    if hop + 1 < length - 1:
                        @pl.when(can_send(way, hop + 1))
                        def _():
                            along(way, hop + 1, chunk, block).start()
                    across(way, hop + 1, chunk, block).start()
        for way in range(2):
            @pl.when(arrives(way, hop))
            def _():
                project(origin(way, hop))
        if hop == 0:
            for chunk in range(CHUNKS):
                across(0, 0, chunk, partner).wait_recv()
            project(partner)
    for hop in range(1, length):
        for way in range(2):
            @pl.when(arrives(way, hop - 1))
            def _():
                block = origin(way, hop - 1) + partner - me
                for chunk in range(CHUNKS):
                    across(way, hop, chunk, block).wait_recv()
                project(block)
    own_grads.wait()
    own_docs.wait()
    for copy in small:
        copy.wait()

    numbers = docs_s[...]
    counts = [
        jnp.sum(
            jnp.sum(jnp.where(numbers == d, 1.0, 0.0), axis=0), axis=-1, keepdims=True
        )
        for d in range(DOCS - 1)
    ]

    def first_of(block):
        own = docs_s[block]
        start = jnp.zeros(own.shape, jnp.float32)
        for d in range(DOCS - 1):
            start = start + jnp.where(own > d, counts[d], 0.0)
        return start.astype(jnp.int32)

    def pick(weight_of, block_of, width):
        total = None
        for b in range(n):
            weight = jnp.concatenate([weight_of(b).astype(jnp.bfloat16)] * (width // HEAD), axis=1)
            term = weight * block_of(b)
            total = term if total is None else total + term
        return total

    def grads_of(block):
        return pick(lambda r: chosen[r * n + block], lambda r: grads_s[r], HEAD)

    dk_s[...] = jnp.zeros_like(dk_s)
    dv_s[...] = jnp.zeros_like(dv_s)
    for i in range(n // 2):
        low, high = 2 * i * BLOCK, 2 * (i + 1) * BLOCK
        first = jnp.concatenate([first_of(2 * i), first_of(2 * i + 1)], axis=1)
        last = low + lax.broadcasted_iota(jnp.int32, (1, 2 * BLOCK), 1)
        pos = lax.broadcasted_iota(jnp.int32, (high, 2 * BLOCK), 0)
        q = q_s[low:high, :]
        g = jnp.concatenate([grads_of(2 * i), grads_of(2 * i + 1)], axis=0)
        keys = k_s[:high, :]
        scores = lax.dot_general(keys, q, NT, preferred_element_type=jnp.float32)
        expon = jnp.where(
            (pos >= first) & (pos <= last),
            jnp.exp2(scores * (FACTOR * math.log2(math.e))),
            0.0,
        )
        prob = expon * (1.0 / jnp.sum(expon, axis=0, keepdims=True))
        prob_low = prob.astype(jnp.bfloat16)
        grad_prob = lax.dot_general(v_s[:high, :], g, NT, preferred_element_type=jnp.float32)
        delta = jnp.sum(prob_low.astype(jnp.float32) * grad_prob, axis=0, keepdims=True)
        dscore = (prob * (grad_prob - delta)).astype(jnp.bfloat16)
        dk_s[:high, :] += jnp.dot(dscore, q, preferred_element_type=jnp.float32)
        dv_s[:high, :] += jnp.dot(prob_low, g, preferred_element_type=jnp.float32)
        dq = lax.dot_general(dscore, keys, TN, preferred_element_type=jnp.float32)
        g_s[low:high, :HEAD] = (dq * FACTOR).astype(jnp.bfloat16)
    g_s[:, HEAD : 2 * HEAD] = (dk_s[...] * FACTOR).astype(jnp.bfloat16)
    g_s[:, 2 * HEAD :] = dv_s[...].astype(jnp.bfloat16)

    def stage(r, carry):
        g_send[r] = pick(
            lambda b: chosen[r * n + b], lambda b: g_s[b * BLOCK : (b + 1) * BLOCK, :], 3 * HEAD
        )
        return carry

    lax.fori_loop(0, n, stage, 0)
    own_g = pltpu.make_async_copy(g_send.at[me], g_all.at[me], own_sem.at[4])
    own_g.start()
    sent_g = []
    sent_v = []
    qk, vv = pl.ds(0, 2 * HEAD), pl.ds(2 * HEAD, HEAD)
    for k in range(1, n):
        peer = peers[k - 1]
        sent_g.append(
            remote(g_send.at[peer, :, qk], g_all.at[me, :, qk], gs.at[k - 1], gr.at[k - 1], seq=peer)
        )
        sent_v.append(
            remote(g_send.at[peer, :, vv], g_all.at[me, :, vv], hs.at[k - 1], hr.at[k - 1], seq=peer)
        )
    for copy in sent_g:
        copy.start()

    w_part[...] = (
        lax.dot_general(normed_s[...], g_s[...], TN, preferred_element_type=jnp.float32)
        .astype(jnp.bfloat16)
        .reshape(w_part.shape)
    )
    held, offset = w_part, 0
    for b, (size, halved) in enumerate(sizes):
        other = pl.multiple_of((1 - bits[b]) * size, size) if halved else 0
        mine = pl.multiple_of(bits[b] * size, size) if halved else 0
        send = remote(
            held.at[:, pl.ds(other, size), :], landed[b], ws.at[b], wr.at[b], dp=partners[b]
        )
        send.start()
        send.wait_recv()
        sums[b][...] = (
            held[:, pl.ds(mine, size), :].astype(jnp.float32) + landed[b][...].astype(jnp.float32)
        ).astype(jnp.bfloat16)
        send.wait_send()
        held, offset = sums[b], offset + mine
    size = sizes[-1][0]
    here = pl.ds(pl.multiple_of(offset, size), size)
    own_w = pltpu.make_async_copy(held.at[me], w_all.at[me, here, :], own_sem.at[5])
    own_w.start()
    sent_w = []
    for k in range(1, n):
        copy = remote(
            held.at[peers[k - 1]], w_all.at[me, here, :], ps.at[k - 1], pr.at[k - 1], seq=peers[k - 1]
        )
        copy.start()
        sent_w.append(copy)

    for copy in sent_v:
        copy.start()

    def d_part(j):
        columns = jnp.concatenate(
            [g_all[h, :, j * HEAD : (j + 1) * HEAD] for h in range(HEADS)], axis=1
        )
        return lax.dot_general(
            columns, weights_s[:, j * HEADS * HEAD : (j + 1) * HEADS * HEAD], NT,
            preferred_element_type=jnp.float32,
        )

    own_g.wait()
    for copy in sent_g:
        copy.wait()
    d_s[...] = d_part(0) + d_part(1)
    inverse, unit, _ = normalized(
        pick(lambda b: chosen[me * n + b], lambda b: frames_s[b], frames_s.shape[2]), gain[...]
    )

    def d_input():
        for copy in sent_v:
            copy.wait()
        gained = (d_s[...] + d_part(2)) * gain[...]
        mean = jnp.mean(gained * unit, axis=-1, keepdims=True)
        d_out[...] = (inverse * (gained - unit * mean)).astype(jnp.bfloat16)

    own_w.wait()
    for copy in sent_w:
        copy.wait()
    spread = [b for b in reversed(range(count)) if sizes[b][1]]
    for b in spread:
        size = sizes[b][0]
        here = pl.ds(pl.multiple_of(offset, size), size)
        copy = remote(
            w_all.at[:, here, :], w_all.at[:, here, :], bs.at[b], br.at[b], dp=partners[b]
        )
        copy.start()
        if b == spread[-1]:
            d_input()
        copy.wait()
        offset = offset - bits[b] * size
    if not spread:
        d_input()

    for chunk in range(CHUNKS):
        across(0, 0, chunk, me).wait_send()
        for way in range(2):
            for hop in range(length - 1):
                @pl.when(can_send(way, hop))
                def _():
                    along(way, hop, chunk, me).wait_send()

                @pl.when(arrives(way, hop))
                def _():
                    across(way, hop + 1, chunk, me).wait_send()


def results_kernel(scale, d_in, w_in, d_out, w_out):
    d_out[0] = d_in[...]
    for h in range(HEADS):
        w_out[:, h * HEAD : (h + 1) * HEAD] = w_in[h].astype(jnp.float32) * scale


def results(scale, d_frames, w_all):
    rows, width = d_frames.shape
    n, w_rows, _ = w_all.shape
    return pl.pallas_call(
        functools.partial(results_kernel, scale),
        grid=(3,),
        in_specs=[
            pl.BlockSpec((rows, width), lambda j: (0, 0)),
            pl.BlockSpec((n, w_rows, HEAD), lambda j: (0, 0, j)),
        ],
        out_specs=(
            pl.BlockSpec((1, rows, width), lambda j: (0, 0, 0)),
            pl.BlockSpec((w_rows, HEADS * HEAD), lambda j: (0, j)),
        ),
        out_shape=(
            jax.ShapeDtypeStruct((1, rows, width), jnp.bfloat16),
            jax.ShapeDtypeStruct((w_rows, 3 * HEADS * HEAD), jnp.float32),
        ),
        name="results",
    )(d_frames, w_all)


def body(n, groups, layer_rows, doc_ids, packing, norm_gain, w_qkv, d_attn):
    width = w_qkv.shape[0]
    total = n * BLOCK
    rows = width // n
    sizes = halvings(rows, groups)
    count = len(sizes)
    dma = pltpu.SemaphoreType.DMA
    low = jnp.bfloat16
    hbm = pl.BlockSpec(memory_space=pl.ANY)
    vmem = pl.BlockSpec(memory_space=pltpu.VMEM)
    buffers = [pltpu.VMEM((n, size, 3 * HEAD), low) for size, _ in sizes]
    routes = dma((2, n // 2, CHUNKS))
    d_frames, w_all = pl.pallas_call(
        functools.partial(kernel, n, groups),
        out_shape=(
            jax.ShapeDtypeStruct((BLOCK, width), low),
            jax.ShapeDtypeStruct((n, rows, 3 * HEAD), low),
        ),
        in_specs=[vmem, hbm, vmem, hbm, hbm, hbm],
        out_specs=(vmem, hbm),
        scratch_shapes=[
            pltpu.VMEM((n, BLOCK, width), low),
            pltpu.VMEM((n, 1, BLOCK), jnp.int32),
            pltpu.VMEM((n, BLOCK, HEAD), low),
            pltpu.VMEM(w_qkv.shape, low),
            pltpu.VMEM((total, width), low),
            pltpu.VMEM((total, HEAD), low),
            pltpu.VMEM((total, HEAD), low),
            pltpu.VMEM((total, HEAD), low),
            pltpu.VMEM((total, HEAD), jnp.float32),
            pltpu.VMEM((total, HEAD), jnp.float32),
            pltpu.VMEM((total, 3 * HEAD), low),
            pltpu.VMEM((n, BLOCK, 3 * HEAD), low),
            pltpu.VMEM((n, BLOCK, 3 * HEAD), low),
            pltpu.VMEM((n, rows, 3 * HEAD), low),
            pltpu.VMEM((n * n, 1, HEAD), jnp.float32),
            pltpu.VMEM((BLOCK, width), jnp.float32),
            dma((6,)),
            *buffers, *buffers,
            routes, routes, routes, routes,
            dma((n,)), dma((n,)), dma((n,)), dma((n,)), dma((n,)), dma((n,)),
            dma((n,)), dma((n,)),
            dma((count,)), dma((count,)), dma((n,)), dma((n,)), dma((count,)), dma((count,)),
        ],
        compiler_params=pltpu.CompilerParams(
            collective_id=0, has_side_effects=True, vmem_limit_bytes=VMEM_LIMIT
        ),
        name="attention_backward",
    )(packing, layer_rows[0], norm_gain.reshape(1, -1), w_qkv, doc_ids, d_attn[0])
    return results(1.0 / math.sqrt(total * groups), d_frames, w_all)


def solution(mesh):
    return jax.shard_map(
        functools.partial(body, mesh.shape["seq"], mesh.shape["dp"]),
        mesh=mesh,
        in_specs=(
            P("dp", "seq", None),
            P("dp", "seq"),
            P("dp", None),
            P(),
            P(),
            P("dp", "seq", None),
        ),
        out_specs=(P("dp", "seq", None), P("seq", None)),
        check_vma=False,
    )
```

profile of v0, /device:TPU:0, one launch (start us, length us, event | category | flops | bytes accessed | tf_op | source)
XLA Modules:
  0.0 69.9 jit_solution(13984020955895778076)
XLA Ops:
  0.6 66.1 %attention_backward.1 = (bf16[128,1024]{1,0:T(8,128)(2,1)}, bf16[8,128,384]{2,1,0:T(8,128)(2,1)}) custom-call(s32[1,8]{1,0:T(1,128)} %packing.1, bf16[128,1024]{1,0:T(8,128)(2,1)} %bitcast.3, f32[1,1024]{1,0:T(1,128)} %bitcast.5, bf16[1024,3072]{1,0:T(8,128)(2,1)} %w_qkv.1, s32[1,128]{1,0:T(1,128)} %docs.1, bf16[128,1024]{1,0:T(8,128)(2,1)} %bitcast.4), custom_call_target="tpu_custom_call" | custom-call | tf_op jit(solution)/shard_map/attention_backward/pallas_call | solution.py:384
  66.7 3.2 %results.1 = (bf16[1,128,1024]{2,1,0:T(8,128)(2,1)}, f32[128,3072]{1,0:T(8,128)}) custom-call(bf16[128,1024]{1,0:T(8,128)(2,1)} %get-tuple-element.4.d_in, bf16[8,128,384]{2,1,0:T(8,128)(2,1)} %get-tuple-element.5.w_in), custom_call_target="tpu_custom_call" | custom-call | tf_op jit(solution)/shard_map/results/pallas_call | solution.py:353
where the time goes:
time: 70.1 us; the launch traced here: 69.9 us
  Pallas kernels  69.3 us (99%)
    pallas_call x1, Pallas kernels, body(): pl.pallas_call(functools.partial(kernel, n, groups), out_shape=(jax.Shape...  66.1 us
    pallas_call x1, Pallas kernels, results(): pl.pallas_call(functools.partial(results_kernel, scale), grid=(3,), in_sp...  3.19 us

commit v1 on v0

--- a/solution.py
+++ b/solution.py
@@ -45,13 +45,13 @@
 
 def kernel(
     n, groups, packing, frames, gain, w_qkv, docs, grads, d_out, w_all,
-    frames_s, docs_s, grads_s, weights_s, normed_s, q_s, k_s, v_s, dk_s, dv_s,
-    g_s, g_send, g_all, w_part, chosen, d_s, own_sem, *scratch,
+    frames_s, docs_s, grads_s, weights_s, normed_s, q_s, k_s, v_s, prob_s, dscore_s,
+    packed_s, g_s, g_send, g_all, w_part, chosen, d_s, own_sem, *scratch,
 ):
-    sizes = halvings(w_part.shape[1], groups)
+    sizes = halvings(w_part.shape[2], groups)
     count = len(sizes)
     landed, sums = scratch[:count], scratch[count : 2 * count]
-    zs, zr, ys, yr, ds, dr, ts, tr, gs, gr, hs, hr, ws, wr, ps, pr, bs, br = scratch[2 * count :]
+    zs, zr, ys, yr, ds, dr, ts, tr, gs, gr, ws, wr, ps, pr, bs, br = scratch[2 * count :]
     me = lax.axis_index("seq")
     dp = lax.axis_index("dp")
     side = lax.rem(me, 2)
@@ -120,13 +120,13 @@
         small.append(
             remote(head_of(peers[k - 1]), grads_s.at[me], ts.at[k - 1], tr.at[k - 1], seq=peers[k - 1])
         )
-    for copy in small:
+    for copy in small[::2]:
         copy.start()
 
     def project(block):
         rows = pl.ds(pl.multiple_of(block * BLOCK, BLOCK), BLOCK)
         normed = normalized(frames_s[block], gain[...])[2]
-        normed_s[rows, :] = normed
+        normed_s[:, rows] = normed.T
         for j, kept in enumerate((q_s, k_s, v_s)):
             columns = pl.ds(pl.multiple_of((j * HEADS + head) * HEAD, HEAD), HEAD)
             kept[rows, :] = jnp.dot(
@@ -162,6 +162,8 @@
             for chunk in range(CHUNKS):
                 across(0, 0, chunk, partner).wait_recv()
             project(partner)
+    for copy in small[1::2]:
+        copy.start()
     for hop in range(1, length):
         for way in range(2):
             @pl.when(arrives(way, hop - 1))
@@ -201,8 +203,6 @@
     def grads_of(block):
         return pick(lambda r: chosen[r * n + block], lambda r: grads_s[r], HEAD)
 
-    dk_s[...] = jnp.zeros_like(dk_s)
-    dv_s[...] = jnp.zeros_like(dv_s)
     for i in range(n // 2):
         low, high = 2 * i * BLOCK, 2 * (i + 1) * BLOCK
         first = jnp.concatenate([first_of(2 * i), first_of(2 * i + 1)], axis=1)
@@ -210,6 +210,7 @@
         pos = lax.broadcasted_iota(jnp.int32, (high, 2 * BLOCK), 0)
         q = q_s[low:high, :]
         g = jnp.concatenate([grads_of(2 * i), grads_of(2 * i + 1)], axis=0)
+        packed_s[low:high, :] = g
         keys = k_s[:high, :]
         scores = lax.dot_general(keys, q, NT, preferred_element_type=jnp.float32)
         expon = jnp.where(
@@ -222,110 +223,153 @@
         grad_prob = lax.dot_general(v_s[:high, :], g, NT, preferred_element_type=jnp.float32)
         delta = jnp.sum(prob_low.astype(jnp.float32) * grad_prob, axis=0, keepdims=True)
         dscore = (prob * (grad_prob - delta)).astype(jnp.bfloat16)
-        dk_s[:high, :] += jnp.dot(dscore, q, preferred_element_type=jnp.float32)
-        dv_s[:high, :] += jnp.dot(prob_low, g, preferred_element_type=jnp.float32)
+        prob_s[:high, low:high] = prob_low
+        dscore_s[:high, low:high] = dscore
         dq = lax.dot_general(dscore, keys, TN, preferred_element_type=jnp.float32)
-        g_s[low:high, :HEAD] = (dq * FACTOR).astype(jnp.bfloat16)
-    g_s[:, HEAD : 2 * HEAD] = (dk_s[...] * FACTOR).astype(jnp.bfloat16)
-    g_s[:, 2 * HEAD :] = dv_s[...].astype(jnp.bfloat16)
-
-    def stage(r, carry):
-        g_send[r] = pick(
-            lambda b: chosen[r * n + b], lambda b: g_s[b * BLOCK : (b + 1) * BLOCK, :], 3 * HEAD
-        )
-        return carry
-
-    lax.fori_loop(0, n, stage, 0)
-    own_g = pltpu.make_async_copy(g_send.at[me], g_all.at[me], own_sem.at[4])
-    own_g.start()
-    sent_g = []
-    sent_v = []
-    qk, vv = pl.ds(0, 2 * HEAD), pl.ds(2 * HEAD, HEAD)
-    for k in range(1, n):
-        peer = peers[k - 1]
-        sent_g.append(
-            remote(g_send.at[peer, :, qk], g_all.at[me, :, qk], gs.at[k - 1], gr.at[k - 1], seq=peer)
-        )
-        sent_v.append(
-            remote(g_send.at[peer, :, vv], g_all.at[me, :, vv], hs.at[k - 1], hr.at[k - 1], seq=peer)
-        )
-    for copy in sent_g:
-        copy.start()
-
-    w_part[...] = (
-        lax.dot_general(normed_s[...], g_s[...], TN, preferred_element_type=jnp.float32)
-        .astype(jnp.bfloat16)
-        .reshape(w_part.shape)
-    )
+        g_s[0, low:high, :] = (dq * FACTOR).astype(jnp.bfloat16)
+
+    def key_sums(p, kept, other_of, factor):
+        for j in range(n // 2):
+            low, high = 2 * j * BLOCK, 2 * (j + 1) * BLOCK
+            total = jnp.dot(
+                kept[low:high, low:], other_of(low), preferred_element_type=jnp.float32
+            )
+            g_s[p, low:high, :] = (total * factor).astype(jnp.bfloat16)
+
+    def stage(p):
+        for r in range(n):
+            g_send[p, r] = pick(
+                lambda b: chosen[r * n + b], lambda b: g_s[p, b * BLOCK : (b + 1) * BLOCK, :], HEAD
+            )
+
+    def halve(p, b, held):
+        size, halved = sizes[b]
+        other = pl.multiple_of((1 - bits[b]) * size, size) if halved else 0
+        send = remote(
+            held.at[p, :, pl.ds(other, size), :], landed[b].at[p], ws.at[b, p], wr.at[b, p],
+            dp=partners[b],
+        )
+        send.start()
+        return send
+
+    def weight_part(p):
+        w_part[p] = (
+            jnp.dot(normed_s[...], g_s[p], preferred_element_type=jnp.float32)
+            .astype(jnp.bfloat16)
+            .reshape(w_part.shape[1:])
+        )
+        return halve(p, 0, w_part)
+
+    def grad_copies(p):
+        own_g[p].start()
+        return [
+            remote(
+                g_send.at[p, peer], g_all.at[p, me], gs.at[p, k], gr.at[p, k], seq=peer
+            )
+            for k, peer in enumerate(peers)
+        ]
+
+    own_g = [
+        pltpu.make_async_copy(g_send.at[p, me], g_all.at[p, me], own_sem.at[4 + p]) for p in range(3)
+    ]
+    sent_g, halves = [], []
+    for p in range(3):
+        if p == 1:
+            key_sums(1, dscore_s, lambda low: q_s[low:, :], FACTOR)
+        if p == 2:
+            key_sums(2, prob_s, lambda low: packed_s[low:, :], 1.0)
+        stage(p)
+        sent_g.append(grad_copies(p))
+        if p < 2:
+            for copy in sent_g[p]:
+                copy.start()
+        halves.append(weight_part(p))
+
     held, offset = w_part, 0
     for b, (size, halved) in enumerate(sizes):
-        other = pl.multiple_of((1 - bits[b]) * size, size) if halved else 0
         mine = pl.multiple_of(bits[b] * size, size) if halved else 0
-        send = remote(
-            held.at[:, pl.ds(other, size), :], landed[b], ws.at[b], wr.at[b], dp=partners[b]
-        )
-        send.start()
-        send.wait_recv()
-        sums[b][...] = (
-            held[:, pl.ds(mine, size), :].astype(jnp.float32) + landed[b][...].astype(jnp.float32)
-        ).astype(jnp.bfloat16)
-        send.wait_send()
-        held, offset = sums[b], offset + mine
+        later = []
+        for p in range(3):
+            halves[p].wait_recv()
+            sums[b][p] = (
+                held[p, :, pl.ds(mine, size), :].astype(jnp.float32)
+                + landed[b][p].astype(jnp.float32)
+            ).astype(jnp.bfloat16)
+            if b + 1 < count:
+                later.append(halve(p, b + 1, sums[b]))
+            halves[p].wait_send()
+        halves, held, offset = later, sums[b], offset + mine
     size = sizes[-1][0]
     here = pl.ds(pl.multiple_of(offset, size), size)
-    own_w = pltpu.make_async_copy(held.at[me], w_all.at[me, here, :], own_sem.at[5])
-    own_w.start()
-    sent_w = []
-    for k in range(1, n):
-        copy = remote(
-            held.at[peers[k - 1]], w_all.at[me, here, :], ps.at[k - 1], pr.at[k - 1], seq=peers[k - 1]
-        )
-        copy.start()
-        sent_w.append(copy)
-
-    for copy in sent_v:
+    sent_w, own_w = [], []
+    for p in range(3):
+        own = pltpu.make_async_copy(held.at[p, me], w_all.at[p, me, here, :], own_sem.at[7 + p])
+        own.start()
+        own_w.append(own)
+        sent_w.append([
+            remote(
+                held.at[p, peer], w_all.at[p, me, here, :], ps.at[p, k], pr.at[p, k], seq=peer
+            )
+            for k, peer in enumerate(peers)
+        ])
+        for copy in sent_w[p]:
+            copy.start()
+    for copy in sent_g[2]:
         copy.start()
 
     def d_part(j):
         columns = jnp.concatenate(
-            [g_all[h, :, j * HEAD : (j + 1) * HEAD] for h in range(HEADS)], axis=1
+            [g_all[j, h] for h in range(HEADS)], axis=1
         )
         return lax.dot_general(
             columns, weights_s[:, j * HEADS * HEAD : (j + 1) * HEADS * HEAD], NT,
             preferred_element_type=jnp.float32,
         )
 
-    own_g.wait()
-    for copy in sent_g:
-        copy.wait()
+    for p in range(2):
+        for copy in [own_g[p]] + sent_g[p]:
+            copy.wait()
     d_s[...] = d_part(0) + d_part(1)
     inverse, unit, _ = normalized(
         pick(lambda b: chosen[me * n + b], lambda b: frames_s[b], frames_s.shape[2]), gain[...]
     )
 
     def d_input():
-        for copy in sent_v:
+        for copy in [own_g[2]] + sent_g[2]:
             copy.wait()
         gained = (d_s[...] + d_part(2)) * gain[...]
         mean = jnp.mean(gained * unit, axis=-1, keepdims=True)
         d_out[...] = (inverse * (gained - unit * mean)).astype(jnp.bfloat16)
 
-    own_w.wait()
-    for copy in sent_w:
-        copy.wait()
     spread = [b for b in reversed(range(count)) if sizes[b][1]]
-    for b in spread:
+
+    def widen(p, b, offset):
         size = sizes[b][0]
         here = pl.ds(pl.multiple_of(offset, size), size)
         copy = remote(
-            w_all.at[:, here, :], w_all.at[:, here, :], bs.at[b], br.at[b], dp=partners[b]
+            w_all.at[p, :, here, :], w_all.at[p, :, here, :], bs.at[b, p], br.at[b, p],
+            dp=partners[b],
         )
         copy.start()
-        if b == spread[-1]:
+        return copy
+
+    spreading = []
+    for p in range(3):
+        for copy in [own_w[p]] + sent_w[p]:
+            copy.wait()
+        if spread:
+            spreading.append(widen(p, spread[0], offset))
+    for place_of, b in enumerate(spread):
+        offset = offset - bits[b] * sizes[b][0]
+        later = []
+        for p in range(3):
+            spreading[p].wait()
+            if place_of + 1 < len(spread):
+                later.append(widen(p, spread[place_of + 1], offset))
+        spreading = later
+        if place_of + 2 == len(spread):
             d_input()
-        copy.wait()
-        offset = offset - bits[b] * size
-    if not spread:
+    if len(spread) < 2:
         d_input()
 
     for chunk in range(CHUNKS):
@@ -344,18 +388,18 @@
 def results_kernel(scale, d_in, w_in, d_out, w_out):
     d_out[0] = d_in[...]
     for h in range(HEADS):
-        w_out[:, h * HEAD : (h + 1) * HEAD] = w_in[h].astype(jnp.float32) * scale
+        w_out[:, h * HEAD : (h + 1) * HEAD] = w_in[0, h].astype(jnp.float32) * scale
 
 
 def results(scale, d_frames, w_all):
     rows, width = d_frames.shape
-    n, w_rows, _ = w_all.shape
+    _, n, w_rows, _ = w_all.shape
     return pl.pallas_call(
         functools.partial(results_kernel, scale),
         grid=(3,),
         in_specs=[
             pl.BlockSpec((rows, width), lambda j: (0, 0)),
-            pl.BlockSpec((n, w_rows, HEAD), lambda j: (0, 0, j)),
+            pl.BlockSpec((1, n, w_rows, HEAD), lambda j: (j, 0, 0, 0)),
         ],
         out_specs=(
             pl.BlockSpec((1, rows, width), lambda j: (0, 0, 0)),
@@ -379,13 +423,13 @@
     low = jnp.bfloat16
     hbm = pl.BlockSpec(memory_space=pl.ANY)
     vmem = pl.BlockSpec(memory_space=pltpu.VMEM)
-    buffers = [pltpu.VMEM((n, size, 3 * HEAD), low) for size, _ in sizes]
+    buffers = [pltpu.VMEM((3, n, size, HEAD), low) for size, _ in sizes]
     routes = dma((2, n // 2, CHUNKS))
     d_frames, w_all = pl.pallas_call(
         functools.partial(kernel, n, groups),
         out_shape=(
             jax.ShapeDtypeStruct((BLOCK, width), low),
-            jax.ShapeDtypeStruct((n, rows, 3 * HEAD), low),
+            jax.ShapeDtypeStruct((3, n, rows, HEAD), low),
         ),
         in_specs=[vmem, hbm, vmem, hbm, hbm, hbm],
         out_specs=(vmem, hbm),
@@ -394,24 +438,24 @@
             pltpu.VMEM((n, 1, BLOCK), jnp.int32),
             pltpu.VMEM((n, BLOCK, HEAD), low),
             pltpu.VMEM(w_qkv.shape, low),
-            pltpu.VMEM((total, width), low),
+            pltpu.VMEM((width, total), low),
             pltpu.VMEM((total, HEAD), low),
             pltpu.VMEM((total, HEAD), low),
             pltpu.VMEM((total, HEAD), low),
-            pltpu.VMEM((total, HEAD), jnp.float32),
-            pltpu.VMEM((total, HEAD), jnp.float32),
-            pltpu.VMEM((total, 3 * HEAD), low),
-            pltpu.VMEM((n, BLOCK, 3 * HEAD), low),
-            pltpu.VMEM((n, BLOCK, 3 * HEAD), low),
-            pltpu.VMEM((n, rows, 3 * HEAD), low),
+            pltpu.VMEM((total, total), low),
+            pltpu.VMEM((total, total), low),
+            pltpu.VMEM((total, HEAD), low),
+            pltpu.VMEM((3, total, HEAD), low),
+            pltpu.VMEM((3, n, BLOCK, HEAD), low),
+            pltpu.VMEM((3, n, BLOCK, HEAD), low),
+            pltpu.VMEM((3, n, rows, HEAD), low),
             pltpu.VMEM((n * n, 1, HEAD), jnp.float32),
             pltpu.VMEM((BLOCK, width), jnp.float32),
-            dma((6,)),
+            dma((10,)),
             *buffers, *buffers,
             routes, routes, routes, routes,
-            dma((n,)), dma((n,)), dma((n,)), dma((n,)), dma((n,)), dma((n,)),
-            dma((n,)), dma((n,)),
-            dma((count,)), dma((count,)), dma((n,)), dma((n,)), dma((count,)), dma((count,)),
+            dma((n,)), dma((n,)), dma((n,)), dma((n,)), dma((3, n)), dma((3, n)),
+            dma((count, 3)), dma((count, 3)), dma((3, n)), dma((3, n)), dma((count, 3)), dma((count, 3)),
         ],
         compiler_params=pltpu.CompilerParams(
             collective_id=0, has_side_effects=True, vmem_limit_bytes=VMEM_LIMIT

time: 70.1 us -> 68.3 us (0.974)
  Pallas kernels: 69.3 us -> 67.4 us
    pallas_call x1, Pallas kernels: 66.1 us -> 64.3 us  [body(): pl.pallas_call(functools.partial(kernel, n, groups), out_shape=(jax.Shape...]
where the time goes in v1:
time: 68.3 us; the launch traced here: 68.1 us
  Pallas kernels  67.4 us (99%)
    pallas_call x1, Pallas kernels, body(): pl.pallas_call(functools.partial(kernel, n, groups), out_shape=(jax.Shape...  64.3 us
    pallas_call x1, Pallas kernels, results(): pl.pallas_call(functools.partial(results_kernel, scale), grid=(3,), in_sp...  3.19 us

profile of v1, /device:TPU:0, one launch (start us, length us, event | category | flops | bytes accessed | tf_op | source)
XLA Modules:
  0.0 68.1 jit_solution(6236697218735295632)
XLA Ops:
  0.6 64.3 %attention_backward.1 = (bf16[128,1024]{1,0:T(8,128)(2,1)}, bf16[3,8,128,128]{3,2,1,0:T(8,128)(2,1)}) custom-call(s32[1,8]{1,0:T(1,128)} %packing.1, bf16[128,1024]{1,0:T(8,128)(2,1)} %bitcast.3, f32[1,1024]{1,0:T(1,128)} %bitcast.5, bf16[1024,3072]{1,0:T(8,128)(2,1)} %w_qkv.1, s32[1,128]{1,0:T(1,128)} %docs.1, bf16[128,1024]{1,0:T(8,128)(2,1)} %bitcast.4), custom_call_target="tpu_custom_call" | custom-call | tf_op jit(solution)/shard_map/attention_backward/pallas_call | solution.py:428
  64.9 3.2 %results.1 = (bf16[1,128,1024]{2,1,0:T(8,128)(2,1)}, f32[128,3072]{1,0:T(8,128)}) custom-call(bf16[128,1024]{1,0:T(8,128)(2,1)} %get-tuple-element.4.d_in, bf16[3,8,128,128]{3,2,1,0:T(8,128)(2,1)} %get-tuple-element.5.w_in), custom_call_target="tpu_custom_call" | custom-call | tf_op jit(solution)/shard_map/results/pallas_call | solution.py:397

commit v2 on v1

--- a/solution.py
+++ b/solution.py
@@ -17,6 +17,7 @@
 MESH = pl.DeviceIdType.MESH
 VMEM_LIMIT = 56 * 1024 * 1024
 CHUNKS = 4
+TWINS = CHUNKS // 2
 NT = (((1,), (1,)), ((), ()))
 TN = (((0,), (0,)), ((), ()))
 
@@ -96,6 +97,12 @@
             ys.at[way, hop, chunk], yr.at[way, hop, chunk], seq=partner,
         )
 
+    def twin(way, chunk):
+        return remote(
+            piece(partner, chunk), piece(partner, chunk),
+            ys.at[way, 1, chunk], yr.at[way, 1, chunk], seq=me + (2 if way == 0 else -2),
+        )
+
     def can_send(way, hop):
         if way == 0:
             return (place + 1 < length) & (place - hop >= 0)
@@ -113,7 +120,8 @@
             @pl.when(can_send(way, 0))
             def _():
                 along(way, 0, chunk, me, source).start()
-        across(0, 0, chunk, me, source).start()
+    for chunk in reversed(range(CHUNKS)):
+        across(0, 0, chunk, me, frames.at[pl.ds(chunk * part, part), :]).start()
     small = []
     for k in range(1, n):
         small.append(remote(docs, docs_s.at[me], ds.at[k - 1], dr.at[k - 1], seq=peers[k - 1]))
@@ -153,13 +161,21 @@
                         @pl.when(can_send(way, hop + 1))
                         def _():
                             along(way, hop + 1, chunk, block).start()
-                    across(way, hop + 1, chunk, block).start()
+                    if hop > 0 or chunk < TWINS:
+                        across(way, hop + 1, chunk, block).start()
+        if hop == 0:
+            for chunk in reversed(range(TWINS, CHUNKS)):
+                across(0, 0, chunk, partner).wait_recv()
+                for way in range(2):
+                    @pl.when(can_send(way, 0))
+                    def _():
+                        twin(way, chunk).start()
         for way in range(2):
             @pl.when(arrives(way, hop))
             def _():
                 project(origin(way, hop))
         if hop == 0:
-            for chunk in range(CHUNKS):
+            for chunk in range(TWINS):
                 across(0, 0, chunk, partner).wait_recv()
             project(partner)
     for copy in small[1::2]:
@@ -380,9 +396,14 @@
                 def _():
                     along(way, hop, chunk, me).wait_send()
 
-                @pl.when(arrives(way, hop))
-                def _():
-                    across(way, hop + 1, chunk, me).wait_send()
+                if hop == 0 and chunk >= TWINS:
+                    @pl.when(can_send(way, 0))
+                    def _():
+                        twin(way, chunk).wait_send()
+                else:
+                    @pl.when(arrives(way, hop))
+                    def _():
+                        across(way, hop + 1, chunk, me).wait_send()
 
 
 def results_kernel(scale, d_in, w_in, d_out, w_out):

time: 68.3 us -> 70.7 us (1.035)
  Pallas kernels: 67.4 us -> 69.9 us
    pallas_call x1, Pallas kernels: 64.3 us -> 66.7 us  [body(): pl.pallas_call(functools.partial(kernel, n, groups), out_shape=(jax.Shape...]
where the time goes in v2:
time: 70.7 us; the launch traced here: 70.5 us
  Pallas kernels  69.9 us (99%)
    pallas_call x1, Pallas kernels, body(): pl.pallas_call(functools.partial(kernel, n, groups), out_shape=(jax.Shape...  66.7 us
    pallas_call x1, Pallas kernels, results(): pl.pallas_call(functools.partial(results_kernel, scale), grid=(3,), in_sp...  3.19 us

profile of v2, /device:TPU:0, one launch (start us, length us, event | category | flops | bytes accessed | tf_op | source)
XLA Modules:
  0.0 70.5 jit_solution(16876002258217053558)
XLA Ops:
  0.6 66.7 %attention_backward.1 = (bf16[128,1024]{1,0:T(8,128)(2,1)}, bf16[3,8,128,128]{3,2,1,0:T(8,128)(2,1)}) custom-call(s32[1,8]{1,0:T(1,128)} %packing.1, bf16[128,1024]{1,0:T(8,128)(2,1)} %bitcast.3, f32[1,1024]{1,0:T(1,128)} %bitcast.5, bf16[1024,3072]{1,0:T(8,128)(2,1)} %w_qkv.1, s32[1,128]{1,0:T(1,128)} %docs.1, bf16[128,1024]{1,0:T(8,128)(2,1)} %bitcast.4), custom_call_target="tpu_custom_call" | custom-call | tf_op jit(solution)/shard_map/attention_backward/pallas_call | solution.py:449
  67.3 3.2 %results.1 = (bf16[1,128,1024]{2,1,0:T(8,128)(2,1)}, f32[128,3072]{1,0:T(8,128)}) custom-call(bf16[128,1024]{1,0:T(8,128)(2,1)} %get-tuple-element.4.d_in, bf16[3,8,128,128]{3,2,1,0:T(8,128)(2,1)} %get-tuple-element.5.w_in), custom_call_target="tpu_custom_call" | custom-call | tf_op jit(solution)/shard_map/results/pallas_call | solution.py:418

commit v3 on v1

--- a/solution.py
+++ b/solution.py
@@ -185,13 +185,6 @@
         for d in range(DOCS - 1)
     ]
 
-    def first_of(block):
-        own = docs_s[block]
-        start = jnp.zeros(own.shape, jnp.float32)
-        for d in range(DOCS - 1):
-            start = start + jnp.where(own > d, counts[d], 0.0)
-        return start.astype(jnp.int32)
-
     def pick(weight_of, block_of, width):
         total = None
         for b in range(n):
@@ -200,18 +193,50 @@
             total = term if total is None else total + term
         return total
 
-    def grads_of(block):
-        return pick(lambda r: chosen[r * n + block], lambda r: grads_s[r], HEAD)
-
-    for i in range(n // 2):
-        low, high = 2 * i * BLOCK, 2 * (i + 1) * BLOCK
-        first = jnp.concatenate([first_of(2 * i), first_of(2 * i + 1)], axis=1)
-        last = low + lax.broadcasted_iota(jnp.int32, (1, 2 * BLOCK), 1)
-        pos = lax.broadcasted_iota(jnp.int32, (high, 2 * BLOCK), 0)
-        q = q_s[low:high, :]
-        g = jnp.concatenate([grads_of(2 * i), grads_of(2 * i + 1)], axis=0)
-        packed_s[low:high, :] = g
-        keys = k_s[:high, :]
+    numbers = numbers.astype(jnp.float32)
+    lane = lax.broadcasted_iota(jnp.int32, (1, BLOCK), 1).astype(jnp.float32)
+    pos = lax.broadcasted_iota(jnp.int32, (n * BLOCK, 2 * BLOCK), 0)
+    firsts, lasts = [], []
+    for b in range(n):
+        start = jnp.zeros((1, BLOCK), jnp.float32)
+        for d in range(DOCS - 1):
+            start = start + jnp.where(numbers[b] > d, counts[d], 0.0)
+        firsts.append(start)
+        lasts.append(lane + b * BLOCK)
+
+    def packed_row(slot, rows):
+        total = jnp.zeros((1, BLOCK), jnp.float32)
+        for b in range(n):
+            total = total + chosen[slot * n + b] * rows[b]
+        return total.astype(jnp.int32)
+
+    def packed_queries(slot):
+        return pick(
+            lambda b: chosen[slot * n + b], lambda b: q_s[b * BLOCK : (b + 1) * BLOCK, :], HEAD
+        )
+
+    def early(it, e, dest):
+        return remote(
+            g_send.at[0, dest], g_all.at[0, me],
+            gs.at[0, 2 * it + e], gr.at[0, 2 * it + (side if it < length - 1 else 0)], seq=dest,
+        )
+
+    def early_landed(it, e):
+        return remote(
+            g_send.at[0, partner], g_all.at[0, partner],
+            gs.at[0, 2 * it + e], gr.at[0, 2 * it + e], seq=partner,
+        )
+
+    keys, sent_q, landed_q = k_s[...], [], []
+    for it in range(length):
+        pair = lax.rem(place + 1 + it, length)
+        slots = (2 * pair, 2 * pair + 1)
+        here = pl.ds(pl.multiple_of(pair * 2 * BLOCK, 2 * BLOCK), 2 * BLOCK)
+        first = jnp.concatenate([packed_row(slot, firsts) for slot in slots], axis=1)
+        last = jnp.concatenate([packed_row(slot, lasts) for slot in slots], axis=1)
+        q = jnp.concatenate([packed_queries(slot) for slot in slots], axis=0)
+        packed_s[here, :] = q
+        g = grads_s[pl.ds(2 * pair, 2)].reshape(2 * BLOCK, HEAD)
         scores = lax.dot_general(keys, q, NT, preferred_element_type=jnp.float32)
         expon = jnp.where(
             (pos >= first) & (pos <= last),
@@ -220,21 +245,28 @@
         )
         prob = expon * (1.0 / jnp.sum(expon, axis=0, keepdims=True))
         prob_low = prob.astype(jnp.bfloat16)
-        grad_prob = lax.dot_general(v_s[:high, :], g, NT, preferred_element_type=jnp.float32)
+        grad_prob = lax.dot_general(v_s[...], g, NT, preferred_element_type=jnp.float32)
         delta = jnp.sum(prob_low.astype(jnp.float32) * grad_prob, axis=0, keepdims=True)
         dscore = (prob * (grad_prob - delta)).astype(jnp.bfloat16)
-        prob_s[:high, low:high] = prob_low
-        dscore_s[:high, low:high] = dscore
+        prob_s[:, here] = prob_low
+        dscore_s[:, here] = dscore
         dq = lax.dot_general(dscore, keys, TN, preferred_element_type=jnp.float32)
-        g_s[0, low:high, :] = (dq * FACTOR).astype(jnp.bfloat16)
-
-    def key_sums(p, kept, other_of, factor):
-        for j in range(n // 2):
-            low, high = 2 * j * BLOCK, 2 * (j + 1) * BLOCK
-            total = jnp.dot(
-                kept[low:high, low:], other_of(low), preferred_element_type=jnp.float32
-            )
-            g_s[p, low:high, :] = (total * factor).astype(jnp.bfloat16)
+        g_send[0, pl.ds(2 * pair, 2)] = (
+            (dq * FACTOR).astype(jnp.bfloat16).reshape(2, BLOCK, HEAD)
+        )
+        if it < length - 1:
+            copies = [early(it, e, slots[e]) for e in range(2)]
+            landed_q.extend(early_landed(it, e) for e in range(2))
+        else:
+            copies = [early(it, 0, partner)]
+            landed_q.append(early_landed(it, 0))
+        for copy in copies:
+            copy.start()
+        sent_q.extend(copies)
+
+    def key_sums(p, kept, other, factor):
+        total = jnp.dot(kept[...], other, preferred_element_type=jnp.float32)
+        g_s[p] = (total * factor).astype(jnp.bfloat16)
 
     def stage(p):
         for r in range(n):
@@ -272,15 +304,22 @@
     own_g = [
         pltpu.make_async_copy(g_send.at[p, me], g_all.at[p, me], own_sem.at[4 + p]) for p in range(3)
     ]
-    sent_g, halves = [], []
+    sent_g, halves = [[]], []
     for p in range(3):
+        if p == 0:
+            own_g[0].start()
+            for b in range(n):
+                g_s[0, b * BLOCK : (b + 1) * BLOCK, :] = pick(
+                    lambda r: chosen[r * n + b], lambda r: g_send[0, r], HEAD
+                )
+        else:
+            if p == 1:
+                key_sums(1, dscore_s, packed_s[...], FACTOR)
+            else:
+                key_sums(2, prob_s, grads_s[...].reshape(n * BLOCK, HEAD), 1.0)
+            stage(p)
+            sent_g.append(grad_copies(p))
         if p == 1:
-            key_sums(1, dscore_s, lambda low: q_s[low:, :], FACTOR)
-        if p == 2:
-            key_sums(2, prob_s, lambda low: packed_s[low:, :], 1.0)
-        stage(p)
-        sent_g.append(grad_copies(p))
-        if p < 2:
             for copy in sent_g[p]:
                 copy.start()
         halves.append(weight_part(p))
@@ -326,6 +365,10 @@
             preferred_element_type=jnp.float32,
         )
 
+    for copy in landed_q:
+        copy.wait_recv()
+    for copy in sent_q:
+        copy.wait_send()
     for p in range(2):
         for copy in [own_g[p]] + sent_g[p]:
             copy.wait()

time: 68.3 us -> 71.7 us (1.050)
  Pallas kernels: 67.4 us -> 70.9 us
    pallas_call x1, Pallas kernels: 64.3 us -> 67.7 us  [body(): pl.pallas_call(functools.partial(kernel, n, groups), out_shape=(jax.Shape...]
where the time goes in v3:
time: 71.7 us; the launch traced here: 71.5 us
  Pallas kernels  70.9 us (99%)
    pallas_call x1, Pallas kernels, body(): pl.pallas_call(functools.partial(kernel, n, groups), out_shape=(jax.Shape...  67.7 us
    pallas_call x1, Pallas kernels, results(): pl.pallas_call(functools.partial(results_kernel, scale), grid=(3,), in_sp...  3.19 us

profile of v3, /device:TPU:0, one launch (start us, length us, event | category | flops | bytes accessed | tf_op | source)
XLA Modules:
  0.0 71.5 jit_solution(6668149254839138988)
XLA Ops:
  0.6 67.7 %attention_backward.1 = (bf16[128,1024]{1,0:T(8,128)(2,1)}, bf16[3,8,128,128]{3,2,1,0:T(8,128)(2,1)}) custom-call(s32[1,8]{1,0:T(1,128)} %packing.1, bf16[128,1024]{1,0:T(8,128)(2,1)} %bitcast.3, f32[1,1024]{1,0:T(1,128)} %bitcast.5, bf16[1024,3072]{1,0:T(8,128)(2,1)} %w_qkv.1, s32[1,128]{1,0:T(1,128)} %docs.1, bf16[128,1024]{1,0:T(8,128)(2,1)} %bitcast.4), custom_call_target="tpu_custom_call" | custom-call | tf_op jit(solution)/shard_map/attention_backward/pallas_call | solution.py:471
  68.3 3.2 %results.1 = (bf16[1,128,1024]{2,1,0:T(8,128)(2,1)}, f32[128,3072]{1,0:T(8,128)}) custom-call(bf16[128,1024]{1,0:T(8,128)(2,1)} %get-tuple-element.4.d_in, bf16[3,8,128,128]{3,2,1,0:T(8,128)(2,1)} %get-tuple-element.5.w_in), custom_call_target="tpu_custom_call" | custom-call | tf_op jit(solution)/shard_map/results/pallas_call | solution.py:440

commit v4 on v1

--- a/solution.py
+++ b/solution.py
@@ -16,7 +16,7 @@
 FACTOR = 1.0 / math.sqrt(HEAD)
 MESH = pl.DeviceIdType.MESH
 VMEM_LIMIT = 56 * 1024 * 1024
-CHUNKS = 4
+CHUNKS = 2
 NT = (((1,), (1,)), ((), ()))
 TN = (((0,), (0,)), ((), ()))
 

time: 68.3 us -> 67.7 us (level)
  no operation moved by 1% of the time
where the time goes in v4:
time: 67.7 us; the launch traced here: 67.5 us
  Pallas kernels  66.8 us (99%)
    pallas_call x1, Pallas kernels, body(): pl.pallas_call(functools.partial(kernel, n, groups), out_shape=(jax.Shape...  63.7 us
    pallas_call x1, Pallas kernels, results(): pl.pallas_call(functools.partial(results_kernel, scale), grid=(3,), in_sp...  3.19 us

profile of v4, /device:TPU:0, one launch (start us, length us, event | category | flops | bytes accessed | tf_op | source)
XLA Modules:
  0.0 67.5 jit_solution(5000742074635832357)
XLA Ops:
  0.6 63.7 %attention_backward.1 = (bf16[128,1024]{1,0:T(8,128)(2,1)}, bf16[3,8,128,128]{3,2,1,0:T(8,128)(2,1)}) custom-call(s32[1,8]{1,0:T(1,128)} %packing.1, bf16[128,1024]{1,0:T(8,128)(2,1)} %bitcast.3, f32[1,1024]{1,0:T(1,128)} %bitcast.5, bf16[1024,3072]{1,0:T(8,128)(2,1)} %w_qkv.1, s32[1,128]{1,0:T(1,128)} %docs.1, bf16[128,1024]{1,0:T(8,128)(2,1)} %bitcast.4), custom_call_target="tpu_custom_call" | custom-call | tf_op jit(solution)/shard_map/attention_backward/pallas_call | solution.py:428
  64.3 3.2 %results.1 = (bf16[1,128,1024]{2,1,0:T(8,128)(2,1)}, f32[128,3072]{1,0:T(8,128)}) custom-call(bf16[128,1024]{1,0:T(8,128)(2,1)} %get-tuple-element.4.d_in, bf16[3,8,128,128]{3,2,1,0:T(8,128)(2,1)} %get-tuple-element.5.w_in), custom_call_target="tpu_custom_call" | custom-call | tf_op jit(solution)/shard_map/results/pallas_call | solution.py:397
